TPU v7x, 128 devices: a whole 4x4x4 slice. The times are simulated.
128 devices in a mesh: kvp: 16 (over z, x), tp: 8 (over y, core).
Axes of the slice: x: 4, y: 4, z: 4, core: 2. Of those that a mesh axis runs over, the one named last changes fastest.
Arguments:
- queries: bfloat16 [4, 128, 4, 128], P(None, 'tp'), may hold values from -128 to 128
- key_cache_rows: bfloat16 [4, 8, 16384, 128], P(None, 'tp', 'kvp'), may hold values from -6 to 6
- value_cache_rows: bfloat16 [4, 8, 16384, 128], P(None, 'tp', 'kvp'), may hold values from -6 to 6
- k_new: bfloat16 [4, 8, 4, 128], P(None, 'tp'), may hold values from -4 to 4
- v_new: bfloat16 [4, 8, 4, 128], P(None, 'tp'), may hold values from -6 to 6
- lengths: int32 [4], replicated, may hold values from 1 to 16365, as said below
- new_owner: int32 [4], replicated, may hold values from 0 to 15, as said below
- residual: bfloat16 [4, 4, 16384], P(None, None, 'kvp'), may hold values from -10 to 10
- norm_gain: float32 [16384], P('kvp'), may hold values from 0.1 to 1.9
- out_weight: bfloat16 [8, 16, 128, 16384], P('tp', 'kvp'), may hold values from -0.0625 to 0.0625
- gate_weight: bfloat16 [16384, 26624], P('kvp', 'tp'), may hold values from -0.046875 to 0.046875
- up_weight: bfloat16 [16384, 26624], P('kvp', 'tp'), may hold values from -0.046875 to 0.046875
- down_weight: bfloat16 [26624, 16384], P('tp', 'kvp'), may hold values from -0.0390625 to 0.0390625
Outputs:
- attended: bfloat16 [4, 8, 16, 4, 128], P(None, 'tp', 'kvp')
- stream_mid: bfloat16 [4, 4, 16384], P(None, None, 'kvp')
- layer_out: bfloat16 [4, 4, 16384], P(None, None, 'kvp')
Inputs may be any that keep to these rules, and one draw needn't show every extreme that they name: `lengths`: some sequence has exactly 16365 cached tokens. `new_owner`: the first two sequences have different owners.
All inputs are finite; a program needn't handle non-finite values.
Results may differ from a plain program's by a relative error of at most 0.011.
Values sent between devices are 32-bit elements; how exact they have to be, the bound alone decides.
No kernel may reach another device: no remote copies, remote signals or barrier semaphores. Data moves between devices by JAX's collectives and lax.ppermute only.
A program may use at most 128 MiB of HBM per device.

v0:
```python
import math

import jax
import jax.numpy as jnp
from jax import lax
from jax.sharding import PartitionSpec as P

D = 16384


neg_large = -1e30
epsilon = 1e-05


def local_partials(queries, key_cache_rows, value_cache_rows, k_new, v_new, lengths, new_owner):
    seq_count, local_kv, slot_count, head_dim = key_cache_rows.shape
    draft_count = k_new.shape[2]
    groups = queries.shape[1] // local_kv
    devices = lax.axis_size("kvp")
    own_index = lax.axis_index("kvp")
    scale_factor_term = 1.0 / math.sqrt(head_dim)
    grouped_query_rows = queries.reshape(seq_count, local_kv, groups * draft_count, head_dim)
    logit_scores = (
        jnp.einsum(
            "sgrd,sgtd->sgrt",
            grouped_query_rows,
            key_cache_rows,
            preferred_element_type=jnp.float32,
        )
        * scale_factor_term
    )
    fresh_scores = (
        jnp.einsum("sgrd,sgid->sgri", grouped_query_rows, k_new, preferred_element_type=jnp.float32)
        * scale_factor_term
    )
    slot_ids = jnp.arange(slot_count, dtype=jnp.int32)
    linear = slot_ids * devices + own_index
    offset = (new_owner - lengths) % devices
    token_pos = linear[None, :] - offset[:, None]
    live_mask = ((token_pos >= 0) & (token_pos < lengths[:, None]))[:, None, None, :]
    draft_ids = jnp.arange(draft_count, dtype=jnp.int32)
    placed = (new_owner[:, None] + draft_ids[None, :]) % devices == own_index
    row_draft = jnp.arange(groups * draft_count, dtype=jnp.int32) % draft_count
    causal = draft_ids[None, :] <= row_draft[:, None]
    fresh_mask = placed[:, None, None, :] & causal[None, None]
    logit_scores = jnp.where(live_mask, logit_scores, neg_large)
    fresh_scores = jnp.where(fresh_mask, fresh_scores, neg_large)
    row_top = jnp.maximum(jnp.max(logit_scores, axis=-1), jnp.max(fresh_scores, axis=-1))
    weights = jnp.where(live_mask, jnp.exp(logit_scores - row_top[..., None]), 0.0)
    fresh_weights = jnp.where(fresh_mask, jnp.exp(fresh_scores - row_top[..., None]), 0.0)
    row_total = jnp.sum(weights, axis=-1) + jnp.sum(fresh_weights, axis=-1)
    weighted_values = jnp.einsum(
        "sgrt,sgtd->sgrd",
        weights.astype(jnp.bfloat16),
        value_cache_rows,
        preferred_element_type=jnp.float32,
    )
    weighted_values = weighted_values + jnp.einsum(
        "sgri,sgid->sgrd",
        fresh_weights.astype(jnp.bfloat16),
        v_new,
        preferred_element_type=jnp.float32,
    )
    part_shape = (seq_count, local_kv, groups, draft_count)
    return (
        weighted_values.reshape(part_shape + (head_dim,)),
        row_top.reshape(part_shape),
        row_total.reshape(part_shape),
    )


def gather_heads(pieces):
    weighted_values, row_top, row_total = pieces
    best_top = jnp.max(row_top, axis=0)
    rescale = jnp.exp(row_top - best_top[None])
    merged_total = jnp.sum(row_total * rescale, axis=0)
    merged = jnp.sum(weighted_values * rescale[..., None], axis=0)
    return (merged / merged_total[..., None]).astype(jnp.bfloat16)


def body(
    queries,
    key_cache_rows,
    value_cache_rows,
    k_new,
    v_new,
    lengths,
    new_owner,
    residual,
    norm_gain,
    out_weight,
    gate_weight,
    up_weight,
    down_weight,
):
    weighted_values, row_top, row_total = local_partials(
        queries, key_cache_rows, value_cache_rows, k_new, v_new, lengths, new_owner
    )
    attended = gather_heads(
        (
            lax.all_to_all(weighted_values[None], "kvp", split_axis=3, concat_axis=0, tiled=True),
            lax.all_to_all(row_top[None], "kvp", split_axis=3, concat_axis=0, tiled=True),
            lax.all_to_all(row_total[None], "kvp", split_axis=3, concat_axis=0, tiled=True),
        )
    )
    seq_count, local_kv, heads_here, draft_count, head_dim = attended.shape
    row_count = seq_count * draft_count
    flat_rows = attended.transpose(0, 3, 1, 2, 4).reshape(
        row_count, local_kv * heads_here * head_dim
    )
    projected = jnp.dot(
        flat_rows,
        out_weight.reshape(local_kv * heads_here * head_dim, out_weight.shape[-1]),
        preferred_element_type=jnp.float32,
    )
    width_here = residual.shape[-1]
    summed = lax.psum(projected, ("kvp", "tp"))
    feature_part = lax.dynamic_slice_in_dim(
        summed, lax.axis_index("kvp") * width_here, width_here, 1
    )
    stream_mid = (
        residual.reshape(row_count, width_here).astype(jnp.float32) + feature_part
    ).astype(jnp.bfloat16)
    wide = stream_mid.astype(jnp.float32)
    squares = lax.psum(jnp.sum(wide * wide, axis=1), "kvp")
    normed = (wide * lax.rsqrt(squares / D + epsilon)[:, None] * norm_gain).astype(jnp.bfloat16)
    gate_part = jnp.dot(normed, gate_weight, preferred_element_type=jnp.float32)
    upper_part = jnp.dot(normed, up_weight, preferred_element_type=jnp.float32)
    gate_full, upper_full = lax.psum((gate_part, upper_part), "kvp")
    active = (jax.nn.silu(gate_full) * upper_full).astype(jnp.bfloat16)
    lowered = lax.psum(jnp.dot(active, down_weight, preferred_element_type=jnp.float32), "tp")
    mixed_rows = (wide + lowered).astype(jnp.bfloat16)
    return (
        attended,
        stream_mid.reshape(seq_count, draft_count, width_here),
        mixed_rows.reshape(seq_count, draft_count, width_here),
    )


def solution(mesh):
    placed = (
        P(None, "tp", None, None),
        P(None, "tp", "kvp", None),
        P(None, "tp", "kvp", None),
        P(None, "tp", None, None),
        P(None, "tp", None, None),
        P(),
        P(),
        P(None, None, "kvp"),
        P("kvp"),
        P("tp", "kvp", None, None),
        P("kvp", "tp"),
        P("kvp", "tp"),
        P("tp", "kvp"),
    )
    return jax.shard_map(
        body,
        mesh=mesh,
        in_specs=placed,
        out_specs=(P(None, "tp", "kvp", None, None), P(None, None, "kvp"), P(None, None, "kvp")),
        check_vma=False,
    )
```

profile of v0, /device:TPU:1, one launch (start us, length us, event | category | flops | bytes accessed | tf_op | source)
XLA Modules:
  0.0 398.0 jit_solution(14644693919145403276)
XLA Ops:
  7.2 0.0 copy-start
  7.2 0.0 copy-start.1
  7.2 0.8 fusion.40
  8.0 0.7 and_select_fusion.2
  8.7 0.7 fusion.23
  9.5 0.0 copy-done
  9.5 0.0 copy-start.2
  9.5 1.4 fusion.45
  10.9 1.0 fusion.46
  11.9 0.1 max.20
  12.0 0.6 copy.17
  12.6 8.4 %all-to-all-start.1 = ((f32[1,4,1,16,4]{4,1,2,0,3:T(4,128)}), f32[1,4,1,16,4]{4,1,2,0,3:T(4,128)S(1)}, u32[]{:S(2)}, u32[]{:S(2)}) async-start(f32[1,4,1,16,4]{4,1,2,0,3:T(4,128)} %copy.17), calls=%async_computation.1 | async-start | bytes 65536 | tf_op jit(solution)/shard_map/all_to_all | solution.py:102
  21.1 0.4 fusion.6
  21.4 1.0 fusion.31
  22.4 1.6 convolution_add_fusion
  24.0 0.1 fusion.29
  24.1 0.1 add.108
  24.2 0.6 copy.18
  24.9 0.7 copy.16
  25.5 2.0 all-to-all-done.1
  27.5 4.6 %all-to-all-start.2 = ((f32[1,4,1,16,4]{4,1,2,0,3:T(4,128)}), f32[1,4,1,16,4]{4,1,2,0,3:T(4,128)S(1)}, u32[]{:S(2)}, u32[]{:S(2)}) async-start(f32[1,4,1,16,4]{4,1,2,0,3:T(4,128)} %copy.18), calls=%async_computation.2 | async-start | bytes 65536 | tf_op jit(solution)/shard_map/all_to_all | solution.py:103
  32.2 6.4 %all-to-all-done.2 = f32[1,4,1,16,4]{4,1,2,0,3:T(4,128)S(1)} async-done(((f32[1,4,1,16,4]{4,1,2,0,3:T(4,128)}), f32[1,4,1,16,4]{4,1,2,0,3:T(4,128)S(1)}, u32[]{:S(2)}, u32[]{:S(2)}) %all-to-all-start.2) | async-done | bytes 1056 | tf_op jit(solution)/shard_map/all_to_all | solution.py:103
  38.6 3.5 all-to-all-start
  42.1 0.0 all-reduce.5.cloned.1.call-start
  42.3 6.7 %all-to-all-done = f32[1,4,1,16,4,128]{5,4,1,2,0,3:T(4,128)S(1)} async-done(((f32[1,4,1,16,4,128]{5,4,1,2,0,3:T(4,128)}), f32[1,4,1,16,4,128]{5,4,1,2,0,3:T(4,128)S(1)}, u32[]{:S(2)}, u32[]{:S(2)}) %all-to-all-start) | async-done | bytes 131104 | tf_op jit(solution)/shard_map/all_to_all | solution.py:101
  48.9 0.1 fusion.12
  49.1 0.1 divide_convert_fusion
  49.2 3.9 fusion
  53.1 0.0 all-reduce.5.cloned.1.call-update
  53.1 0.0 all-reduce.9.cloned.1.call-start
  53.1 0.0 copy-done.1
  53.2 148.3 %all-reduce.5.cloned.1.call-done = f32[16,16384]{1,0:T(8,128)} async-done(((f32[16,16384]{1,0:T(8,128)}), f32[16,16384]{1,0:T(8,128)}) %all-reduce.5.cloned.1.call-update) | async-done | bytes 1048592 | tf_op jit(solution)/shard_map/psum | solution.py:117
  201.5 1.0 fusion.15
  202.5 31.7 %psum.36 = f32[16]{0:T(128)S(1)} all-reduce(f32[16]{0:T(128)S(1)} %get-tuple-element.5), channel_id=1, replica_groups=mesh['kvp'=16,'tp'=8] {'kvp'}, use_global_device_ids=true, to_apply=%region_9.10 | all-reduce | flops 16 | bytes 128 | tf_op jit(solution)/shard_map/psum | solution.py:125
  234.2 0.0 copy-done.2
  234.2 4.7 %fusion.27 = f32[16,3328]{1,0:T(8,128)} fusion(bf16[1024,3328]{1,0:T(8,128)(2,1)} %param.23, bf16[16,1024]{1,0:T(8,128)(2,1)S(1)} %get-tuple-element.6, f32[1024]{0:T(1024)S(1)} %copy-done.2, f32[16]{0:T(128)S(1)} %add_rsqrt_fusion), kind=kOutput, calls=%fused_computation.43 | convolution fusion | flops 109117440 | bytes 7065664 | tf_op jit(solution)/shard_map/dot_general | solution.py:127
  238.9 4.7 %fusion.25 = f32[16,3328]{1,0:T(8,128)} fusion(bf16[1024,3328]{1,0:T(8,128)(2,1)} %param.24, bf16[16,1024]{1,0:T(8,128)(2,1)S(1)} %get-tuple-element.6, f32[1024]{0:T(1024)S(1)} %copy-done.2, f32[16]{0:T(128)S(1)} %add_rsqrt_fusion), kind=kOutput, calls=%fused_computation.42 | convolution fusion | flops 109117440 | bytes 7065664 | tf_op jit(solution)/shard_map/dot_general | solution.py:128
  243.5 0.0 all-reduce.9.cloned.1.call-update
  243.5 0.0 all-reduce.7.cloned.1.call-start
  243.6 84.8 %all-reduce.9.cloned.1.call-done = (f32[16,3328]{1,0:T(8,128)}, f32[16,3328]{1,0:T(8,128)}) async-done(((f32[16,3328]{1,0:T(8,128)}, f32[16,3328]{1,0:T(8,128)}), (f32[16,3328]{1,0:T(8,128)}, f32[16,3328]{1,0:T(8,128)})) %all-reduce.9.cloned.1.call-update) | async-done | bytes 426000 | tf_op jit(solution)/shard_map/psum | solution.py:129
  328.4 4.8 %fusion.13 = f32[16,1024]{1,0:T(8,128)} fusion(bf16[3328,1024]{1,0:T(8,128)(2,1)} %param.25, f32[16,3328]{1,0:T(8,128)} %get-tuple-element.3, f32[16,3328]{1,0:T(8,128)} %get-tuple-element.4), kind=kOutput, calls=%fused_computation.18 | convolution fusion | flops 109371392 | bytes 7307264 | tf_op jit(solution)/shard_map/dot_general | solution.py:131
  333.2 0.0 all-reduce.7.cloned.1.call-update
  333.2 0.7 fusion.24
  333.9 0.6 reshape.340
  334.5 55.5 %all-reduce.7.cloned.1.call-done = f32[16,1024]{1,0:T(8,128)} async-done(((f32[16,1024]{1,0:T(8,128)}), f32[16,1024]{1,0:T(8,128)}) %all-reduce.7.cloned.1.call-update) | async-done | bytes 65552 | tf_op jit(solution)/shard_map/psum | solution.py:131
  390.0 0.8 fusion.18
  390.8 0.6 reshape.341
  (10 shorter events, 0.1 us)
Async XLA Ops:
  7.2 2.3 copy-start
  7.2 46.0 %copy-start.1 = (bf16[4,4,1024]{2,1,0:T(4,128)(2,1)S(1)}, bf16[4,4,1024]{2,1,0:T(4,128)(2,1)}, u32[]{:S(2)}) copy-start(bf16[4,4,1024]{2,1,0:T(4,128)(2,1)} %param.20) | copy-start | bytes 98308
  9.5 224.7 %copy-start.2 = (f32[1024]{0:T(1024)S(1)}, f32[1024]{0:T(1024)}, u32[]{:S(2)}) copy-start(f32[1024]{0:T(1024)} %param.21) | copy-start | bytes 12292
  12.6 14.9 %all-to-all-start.1 = ((f32[1,4,1,16,4]{4,1,2,0,3:T(4,128)}), f32[1,4,1,16,4]{4,1,2,0,3:T(4,128)S(1)}, u32[]{:S(2)}, u32[]{:S(2)}) async-start(f32[1,4,1,16,4]{4,1,2,0,3:T(4,128)} %copy.17), calls=%async_computation.1 | async-start | bytes 65536 | tf_op jit(solution)/shard_map/all_to_all | solution.py:102
  27.5 11.1 %all-to-all-start.2 = ((f32[1,4,1,16,4]{4,1,2,0,3:T(4,128)}), f32[1,4,1,16,4]{4,1,2,0,3:T(4,128)S(1)}, u32[]{:S(2)}, u32[]{:S(2)}) async-start(f32[1,4,1,16,4]{4,1,2,0,3:T(4,128)} %copy.18), calls=%async_computation.2 | async-start | bytes 65536 | tf_op jit(solution)/shard_map/all_to_all | solution.py:103
  38.6 10.3 %all-to-all-start = ((f32[1,4,1,16,4,128]{5,4,1,2,0,3:T(4,128)}), f32[1,4,1,16,4,128]{5,4,1,2,0,3:T(4,128)S(1)}, u32[]{:S(2)}, u32[]{:S(2)}) async-start(f32[1,4,1,16,4,128]{5,4,1,2,0,3:T(4,128)} %copy.16), calls=%async_computation | async-start | bytes 262144 | tf_op jit(solution)/shard_map/all_to_all | solution.py:101
  42.1 159.3 %all-reduce.5.cloned.1.call-start = ((), (), s32[]{:S(2)}) async-start(), calls=%async_computation.3 | async-start | bytes 2097152 | tf_op jit(solution)/shard_map/psum | solution.py:117
  53.1 275.3 %all-reduce.9.cloned.1.call-start = ((), (), s32[]{:S(2)}) async-start(), calls=%async_computation.5 | async-start | bytes 851968 | tf_op jit(solution)/shard_map/psum | solution.py:129
  243.5 146.4 %all-reduce.7.cloned.1.call-start = ((), (), s32[]{:S(2)}) async-start(), calls=%async_computation.4 | async-start | bytes 131072 | tf_op jit(solution)/shard_map/psum | solution.py:131
Sparse Core Ops, SparseCore 0:
  53.2 148.2 all-reduce.4
  243.7 84.6 all-reduce.8
  333.3 56.6 all-reduce.6
where the time goes:
time: 400 us; the launch traced here: 398 us
  waiting for transfers between devices  304 us (76%)
  blocking collectives  31.7 us (8%)
  matrix products  23 us (6%)
  starting transfers between devices  16.7 us (4%)
  between operations  13.9 us (3%)
  other arithmetic  5.49 us (1%)
    psum x1, waiting for transfers between devices, body(): summed = lax.psum(projected, ('kvp', 'tp'))  148 us
    psum x1, waiting for transfers between devices, body(): gate_full, upper_full = lax.psum((gate_part, upper_part), 'kvp')  84.8 us
    psum x1, waiting for transfers between devices, body(): lax.psum(jnp.dot(active, down_weight, preferred_element_type=jnp.float32)...  55.5 us
    psum x1, blocking collectives, body(): squares = lax.psum(jnp.sum(wide * wide, axis=1), 'kvp')  31.7 us
    all_to_all x1, starting transfers between devices, body(): lax.all_to_all(row_top[None], 'kvp', split_axis=3, concat_axis=0, tiled=T...  8.43 us
  transfers between devices with their start and end apart: 6, of which 6 were waited for; matrix products, arithmetic and copies ran while one was open for 1% of the time, Pallas kernels for 0%

commit v1 on v0

v1 whole, which is shorter than its diff:
```python
import math

import jax
import jax.numpy as jnp
from jax import lax
from jax.experimental import pallas as pl
from jax.experimental.pallas import tpu as pltpu
from jax.sharding import PartitionSpec as P

D = 16384
KVP = 16
TP = 8
NEG_LARGE = -1e30
TOP_FLOOR = -1e29
EPSILON = 1e-05
VMEM_LIMIT = 12 * 1024 * 1024
FLOPS = 10**10

F32 = jnp.float32
BF16 = jnp.bfloat16


def exchange(blocks, axis):
    return lax.all_to_all(blocks, axis, split_axis=0, concat_axis=0, tiled=True)


def permute(value, pairs):
    return lax.ppermute(value, "tp", pairs)


def swap_cores(value):
    return permute(value, [(i, i ^ 1) for i in range(TP)])


def half_here():
    tp = lax.axis_index("tp")
    return (tp + (tp >> 1)) & 1


def along_y(value):
    return [permute(value, [(i, i ^ mask) for i in range(TP)]) for mask in (3, 4, 7)]


def call(kernel, outs, args, scratch=(), flops=0, memory=pltpu.VMEM, limit=VMEM_LIMIT):
    moved = sum(math.prod(a.shape) * a.dtype.itemsize for a in list(args) + list(outs))
    return pl.pallas_call(
        kernel,
        out_shape=tuple(outs),
        in_specs=[pl.BlockSpec(memory_space=memory)] * len(args),
        out_specs=tuple(pl.BlockSpec(memory_space=pltpu.VMEM) for _ in outs),
        scratch_shapes=list(scratch),
        compiler_params=pltpu.CompilerParams(vmem_limit_bytes=limit),
        cost_estimate=pl.CostEstimate(flops=flops, bytes_accessed=moved, transcendentals=0),
    )(*args)


def shaped(shape, dtype=F32):
    return jax.ShapeDtypeStruct(shape, dtype)


def attention_kernel(*refs):
    sources, packed, copies, sems = refs[:7], refs[7], refs[8:15], refs[15]
    len_ref, own_ref, q_ref, kn_ref, vn_ref, k_ref, v_ref = copies
    seqs, slots, dim = k_ref.shape
    news = kn_ref.shape[0]
    drafts = news // seqs
    rows = q_ref.shape[0] // seqs
    small = [pltpu.make_async_copy(sources[i], copies[i], sems.at[i]) for i in range(5)]
    keys = [
        pltpu.make_async_copy(sources[5].at[s], k_ref.at[s], sems.at[5 + s]) for s in range(seqs)
    ]
    values = [
        pltpu.make_async_copy(sources[6].at[s], v_ref.at[s], sems.at[5 + seqs + s])
        for s in range(seqs)
    ]
    for copy in keys + small + values:
        copy.start()
    kvp = lax.axis_index("kvp")
    exponent = math.log2(math.e) / math.sqrt(dim)
    linear = lax.broadcasted_iota(jnp.int32, (1, slots), 1) * KVP + kvp
    new_id = lax.broadcasted_iota(jnp.int32, (rows, news), 1)
    row_draft = lax.broadcasted_iota(jnp.int32, (rows, news), 0) % drafts
    lane = lax.broadcasted_iota(jnp.int32, (rows, dim), 1)
    contract = (((1,), (1,)), ((), ()))
    for copy in small + keys:
        copy.wait()
    stats, weights, fresh_weights = [], [], []
    for s in range(seqs):
        length, owner = len_ref[s], own_ref[s]
        offset = (owner - length) & (KVP - 1)
        position = linear - offset
        live = (position >= 0) & (position < length)
        draft = new_id - drafts * s
        fresh = (draft >= 0) & (draft <= row_draft) & (((owner + draft) & (KVP - 1)) == kvp)
        q = q_ref[rows * s : rows * (s + 1), :]
        fresh_scores = lax.dot_general(q, kn_ref[...], contract, preferred_element_type=F32)
        scores = lax.dot_general(q, k_ref[s], contract, preferred_element_type=F32)
        scores = jnp.where(live, scores, NEG_LARGE)
        fresh_scores = jnp.where(fresh, fresh_scores, NEG_LARGE)
        top = jnp.maximum(
            jnp.max(scores, axis=1, keepdims=True), jnp.max(fresh_scores, axis=1, keepdims=True)
        )
        top = jnp.maximum(top, TOP_FLOOR)
        weight = jnp.exp2((scores - top) * exponent)
        fresh_weight = jnp.exp2((fresh_scores - top) * exponent)
        total = jnp.sum(weight, axis=1, keepdims=True)
        total = total + jnp.sum(fresh_weight, axis=1, keepdims=True)
        weights.append(weight.astype(BF16))
        fresh_weights.append(fresh_weight.astype(BF16))
        at = 2 * (s // 2)
        top = top * exponent
        stats.append(jnp.where(lane == at, top, jnp.where(lane == at + 1, total, 0.0)))
    for copy in values:
        copy.wait()
    for s in range(seqs):
        sums = jnp.dot(weights[s], v_ref[s], preferred_element_type=F32)
        sums = sums + jnp.dot(fresh_weights[s], vn_ref[...], preferred_element_type=F32)
        for h in range(rows // drafts):
            packed[h, drafts * s : drafts * (s + 1), :] = sums[drafts * h : drafts * (h + 1), :]
    for part in range(2):
        both = stats[part] + stats[part + 2]
        base = 16 + drafts * part
        for h in range(rows // drafts):
            packed[h, base : base + drafts, :] = both[drafts * h : drafts * (h + 1), :]


def project(att, w_ref, out_ref, half):
    width = out_ref.shape[-1]
    for k in range(KVP):
        start = pl.multiple_of((2 * k + half) * width, width)
        out_ref[k] = jnp.dot(att, w_ref[:, pl.ds(start, width)], preferred_element_type=F32)


def project_other_kernel(parts, w_ref, att_ref, out_ref):
    halves = []
    for half in range(2):
        tops = parts[:, 16:24, 2 * half : 2 * half + 1]
        totals = parts[:, 16:24, 2 * half + 1 : 2 * half + 2]
        scales = jnp.exp2(tops - jnp.max(tops, axis=0, keepdims=True))
        total = jnp.sum(totals * scales, axis=0)
        sums = jnp.sum(parts[:, 8 * half : 8 * half + 8, :] * scales, axis=0)
        halves.append(sums / total)
    att = jnp.concatenate(halves, axis=0).astype(BF16)
    att_ref[...] = att
    project(att, w_ref, out_ref, 1 - half_here())


def project_own_kernel(att_ref, w_ref, out_ref):
    project(att_ref[...], w_ref, out_ref, half_here())


def add_kernel(a, b, out):
    out[...] = a[...] + b[...]


def sum_kernel(parts, out):
    out[...] = jnp.sum(parts[...], axis=0)


def sum_y_kernel(own, one, two, three, out):
    out[...] = (own[...] + two[...]) + (one[...] + three[...])


def joined(own, got):
    first = half_here() == 0
    mine, theirs = own[...], got[...]
    return jnp.concatenate(
        [jnp.where(first, mine, theirs), jnp.where(first, theirs, mine)], axis=1
    )


def widened(added, res_ref, half):
    width = added.shape[1]
    residual = jnp.concatenate(
        [
            jnp.where(half == 0, rows[:, :width], rows[:, width:])
            for rows in (res_ref[s].astype(F32) for s in range(res_ref.shape[0]))
        ],
        axis=0,
    )
    return (residual + added[...]).astype(BF16).astype(F32)


def scaled(wide, gain_ref, half):
    width = wide.shape[1]
    gain = jnp.where(half == 0, gain_ref[:, :width], gain_ref[:, width:])
    return (wide * gain).astype(BF16)


def half_rows(w_ref, half, columns):
    width = w_ref.shape[0] // 2
    return w_ref[pl.ds(pl.multiple_of(half * width, width), width), columns]


def gate_up_own_kernel(own, res_ref, gain_ref, gate_ref, up_ref, wide_ref, gate_out, up_out):
    half = half_here()
    wide = widened(own, res_ref, half)
    wide_ref[...] = wide
    inputs = scaled(wide, gain_ref, half)
    for column in range(0, gate_ref.shape[1], 256):
        columns = slice(column, column + 256)
        for w_ref, out in ((gate_ref, gate_out), (up_ref, up_out)):
            out[:, columns] = jnp.dot(
                inputs, half_rows(w_ref, half, columns), preferred_element_type=F32
            )


def gate_up_other_kernel(
    got, mine_ref, res_ref, gain_ref, gate_ref, up_ref, gate_own, up_own, wide_ref, out
):
    half = 1 - half_here()
    theirs, mine = widened(got, res_ref, half), mine_ref[...]
    wide_ref[...] = jnp.concatenate(
        [jnp.where(half == 1, mine, theirs), jnp.where(half == 1, theirs, mine)], axis=1
    )
    squares = jnp.sum(mine * mine + theirs * theirs, axis=1, keepdims=True)
    inputs = scaled(theirs, gain_ref, half)
    last = []
    for block in range(13):
        columns = slice(256 * block, 256 * (block + 1))
        for start, w_ref, own in ((0, gate_ref, gate_own), (384, up_ref, up_own)):
            part = own[:, columns] + jnp.dot(
                inputs, half_rows(w_ref, half, columns), preferred_element_type=F32
            )
            if block == 12:
                last.append(part)
                continue
            for side in range(2):
                pair, at = divmod(2 * block + side, 3)
                at = start + 128 * at
                for r in range(2):
                    out[2 * pair + r, :, at : at + 128] = part[
                        8 * r : 8 * r + 8, 128 * side : 128 * (side + 1)
                    ]
    spread = jnp.broadcast_to(squares, (mine.shape[0], 64))
    for pair in range(KVP // 2):
        columns = slice(32 * pair, 32 * (pair + 1))
        mixed = jnp.concatenate([last[0][:, columns], last[1][:, columns], spread], axis=1)
        for r in range(2):
            out[2 * pair + r, :, 768:896] = mixed[8 * r : 8 * r + 8]


def gated(gate, up):
    active = gate / (1.0 + jnp.exp(-gate)) * up
    return active.astype(BF16).astype(F32)


def active_kernel(parts, out):
    total = jnp.sum(parts[...], axis=0)
    mixed = total[:, 768:896]
    factor = lax.rsqrt(mixed[:, 64:65] / D + EPSILON)
    active = gated(total[:, :384] * factor, total[:, 384:768] * factor)
    extra = gated(mixed[:, :32] * factor, mixed[:, 32:64] * factor)
    extra = jnp.concatenate([extra, jnp.zeros((8, 96), F32)], axis=1)
    for i in range(out.shape[0]):
        out[i, :, :384] = active
        out[i, :, 384:] = extra


def down(active, w_ref, out, half):
    width = out.shape[1]
    for column in range(0, width, 256):
        start = pl.multiple_of(half * width + column, 256)
        out[:, column : column + 256] = jnp.dot(
            active, w_ref[:, pl.ds(start, 256)], preferred_element_type=F32
        )


def down_other_kernel(parts, w_ref, active_ref, out):
    halves = []
    for r in range(2):
        pairs = [parts[2 * p + r] for p in range(KVP // 2)]
        columns = [p[:, :384] for p in pairs] + [p[:, 384:416] for p in pairs]
        halves.append(jnp.concatenate(columns, axis=1))
    active = jnp.concatenate(halves, axis=0).astype(BF16)
    active_ref[...] = active
    down(active, w_ref, out, 1 - half_here())


def down_own_kernel(active_ref, w_ref, out):
    down(active_ref[...], w_ref, out, half_here())


def finish_kernel(own, got, wide_ref, att_ref, att_out, mid_out, out):
    lowered = joined(own, got)
    wide = wide_ref[...]
    total = wide + lowered
    att_out[...] = att_ref[...]
    seqs, drafts, _ = out.shape
    for s in range(seqs):
        mid_out[s] = wide[drafts * s : drafts * (s + 1)].astype(BF16)
        out[s] = total[drafts * s : drafts * (s + 1)].astype(BF16)


def body(
    queries,
    key_cache_rows,
    value_cache_rows,
    k_new,
    v_new,
    lengths,
    new_owner,
    residual,
    norm_gain,
    out_weight,
    gate_weight,
    up_weight,
    down_weight,
):
    seqs, heads, drafts, dim = queries.shape
    slots = key_cache_rows.shape[2]
    rows, width = seqs * drafts, residual.shape[-1]
    half = width // 2

    in_hbm = [
        pltpu.with_memory_space_constraint(x, pltpu.HBM)
        for x in (
            lengths,
            new_owner,
            queries.reshape(seqs * heads * drafts, dim),
            k_new.reshape(rows, dim),
            v_new.reshape(rows, dim),
            key_cache_rows.reshape(seqs, slots, dim),
            value_cache_rows.reshape(seqs, slots, dim),
        )
    ]
    (parts,) = call(
        attention_kernel,
        [shaped((KVP, 24, dim))],
        in_hbm,
        scratch=[
            pltpu.SMEM((seqs,), jnp.int32),
            pltpu.SMEM((seqs,), jnp.int32),
            pltpu.VMEM((seqs * heads * drafts, dim), BF16),
            pltpu.VMEM((rows, dim), BF16),
            pltpu.VMEM((rows, dim), BF16),
            pltpu.VMEM((seqs, slots, dim), BF16),
            pltpu.VMEM((seqs, slots, dim), BF16),
            pltpu.SemaphoreType.DMA((5 + 2 * seqs,)),
        ],
        flops=FLOPS,
        memory=pltpu.HBM,
    )
    parts = exchange(parts, "kvp")
    weight = out_weight.reshape(dim, -1)
    chunks = shaped((KVP, rows, half))
    flat_rows, theirs = call(
        project_other_kernel, [shaped((rows, dim), BF16), chunks], [parts, weight], flops=FLOPS
    )
    got = swap_cores(theirs)
    (mine,) = call(project_own_kernel, [chunks], [flat_rows, weight], flops=FLOPS)
    (parts,) = call(add_kernel, [chunks], [mine, got], flops=FLOPS)
    (part,) = call(sum_kernel, [shaped((rows, half))], [exchange(parts, "kvp")], flops=FLOPS)
    piece, full = shaped((rows, half)), shaped((rows, width))
    (part,) = call(sum_y_kernel, [piece], [part, *along_y(part)], flops=FLOPS)
    got = swap_cores(part)
    gain, hidden = norm_gain.reshape(1, width), shaped((rows, gate_weight.shape[1]))
    mine, gate_own, up_own = call(
        gate_up_own_kernel,
        [piece, hidden, hidden],
        [part, residual, gain, gate_weight, up_weight],
        flops=FLOPS,
    )
    wide, parts = call(
        gate_up_other_kernel,
        [full, shaped((KVP, 8, 896))],
        [got, mine, residual, gain, gate_weight, up_weight, gate_own, up_own],
        flops=FLOPS,
    )
    (parts,) = call(
        active_kernel, [shaped((KVP, 8, 512))], [exchange(parts, "kvp")], flops=FLOPS
    )
    active, theirs = call(
        down_other_kernel,
        [shaped((rows, down_weight.shape[0]), BF16), piece],
        [exchange(parts, "kvp"), down_weight],
        flops=FLOPS,
    )
    got = swap_cores(theirs)
    (lowered,) = call(down_own_kernel, [piece], [active, down_weight], flops=FLOPS)
    (lowered,) = call(add_kernel, [piece], [lowered, got])
    (lowered,) = call(sum_y_kernel, [piece], [lowered, *along_y(lowered)])
    attended, stream_mid, layer_out = call(
        finish_kernel,
        [
            shaped((rows, dim), BF16),
            shaped((seqs, drafts, width), BF16),
            shaped((seqs, drafts, width), BF16),
        ],
        [lowered, swap_cores(lowered), wide, flat_rows],
    )
    return attended.reshape(seqs, 1, 1, drafts, dim), stream_mid, layer_out


def solution(mesh):
    placed = (
        P(None, "tp", None, None),
        P(None, "tp", "kvp", None),
        P(None, "tp", "kvp", None),
        P(None, "tp", None, None),
        P(None, "tp", None, None),
        P(),
        P(),
        P(None, None, "kvp"),
        P("kvp"),
        P("tp", "kvp", None, None),
        P("kvp", "tp"),
        P("kvp", "tp"),
        P("tp", "kvp"),
    )
    return jax.shard_map(
        body,
        mesh=mesh,
        in_specs=placed,
        out_specs=(P(None, "tp", "kvp", None, None), P(None, None, "kvp"), P(None, None, "kvp")),
        check_vma=False,
    )
```

time: 400 us -> 84.4 us (0.21)
  waiting for transfers between devices: 304 us -> 8.06 us
  matrix products: 23 us -> 0 us
  blocking collectives: 31.7 us -> 53.2 us
  between operations: 13.9 us -> 0.79 us
  Pallas kernels: 0 us -> 7.56 us
  other arithmetic: 5.49 us -> 0.01 us
    psum x3 -> x0, waiting for transfers between devices: 289 us -> none  [the longest x1 148 us: body(): summed = lax.psum(projected, ('kvp', 'tp'))]
    all_to_all x0 -> x4, blocking collectives: none -> 53.2 us  [exchange(): return lax.all_to_all(blocks, axis, split_axis=0, concat_axis=0, tiled=True)]
    psum x1 -> x0, blocking collectives: 31.7 us -> none  [body(): squares = lax.psum(jnp.sum(wide * wide, axis=1), 'kvp')]
    dot_general x8 -> x0, matrix products: 23 us -> none  [the longest x1 4.79 us: body(): jnp.dot(active, down_weight, preferred_element_type=jnp.float32)]
    all_to_all x3 -> x0, starting transfers between devices: 16.6 us -> none  [the longest x1 8.43 us: body(): lax.all_to_all(row_top[None], 'kvp', split_axis=3, concat_axis=0, tiled=T...]
    all_to_all x3 -> x0, waiting for transfers between devices: 15.1 us -> none  [the longest x1 6.69 us: body(): lax.all_to_all(weighted_values[None], 'kvp', split_axis=3, concat_axis=0,...]
    ppermute x0 -> x10, starting transfers between devices: none -> 14.5 us  [permute(): return lax.ppermute(value, 'tp', pairs)]
    ppermute x0 -> x10, waiting for transfers between devices: none -> 8.06 us  [permute(): return lax.ppermute(value, 'tp', pairs)]
  transfers between devices with their start and end apart: 6 -> 10, of which waited for: 6 -> 9; matrix products, arithmetic and copies ran while one was open for 1% -> 0% of each run, Pallas kernels for 0% -> 2%
where the time goes in v1:
time: 84.4 us; the launch traced here: 84.2 us
  blocking collectives  53.2 us (63%)
  starting transfers between devices  14.5 us (17%)
  waiting for transfers between devices  8.06 us (10%)
  Pallas kernels  7.56 us (9%)
    all_to_all x4, blocking collectives, exchange(): return lax.all_to_all(blocks, axis, split_axis=0, concat_axis=0, tiled=True)  53.2 us
    ppermute x10, starting transfers between devices, permute(): return lax.ppermute(value, 'tp', pairs)  14.5 us
    ppermute x10, waiting for transfers between devices, permute(): return lax.ppermute(value, 'tp', pairs)  8.06 us
    pallas_call x14, Pallas kernels, call(): pl.pallas_call(kernel, out_shape=tuple(outs), in_specs=[pl.BlockSpec(memo...  7.56 us
  transfers between devices with their start and end apart: 10, of which 9 were waited for; matrix products, arithmetic and copies ran while one was open for 0% of the time, Pallas kernels for 2%

profile of v1, /device:TPU:1, one launch (start us, length us, event | category | flops | bytes accessed | tf_op | source)
XLA Modules:
  0.0 84.2 jit_solution(1806754759540465481)
XLA Ops:
  0.6 0.0 copy-start
  0.6 2.5 %shard_map.148 = f32[16,24,128]{2,1,0:T(8,128)S(1)} custom-call(s32[4]{0:T(128)} %refs_0_.1, s32[4]{0:T(128)} %refs_1_.1, bf16[256,128]{1,0:T(8,128)(2,1)} %bitcast.22, bf16[16,128]{1,0:T(8,128)(2,1)} %bitcast.23, bf16[16,128]{1,0:T(8,128)(2,1)} %bitcast.24, bf16[4,1024,128]{2,1,0:T(8,128)(2,1)} %bitcast.20, bf16[4,1024,128]{2,1,0:T(8,128)(2,1)} %bitcast.21), custom_call_target="tpu_custom_call" | custom-call | flops 10000000000 | bytes 2367520 | tf_op jit(solution)/shard_map/pallas_call | solution.py:46
  3.1 15.4 %all_to_all.20.parts = f32[16,24,128]{2,1,0:T(8,128)S(1)} all-to-all(f32[16,24,128]{2,1,0:T(8,128)S(1)} %shard_map.148), channel_id=1, replica_groups=mesh['kvp'=16,'tp'=8] {'kvp'}, dimensions={0} | all-to-all | bytes 393216 | tf_op jit(solution)/shard_map/all_to_all | solution.py:24
  18.5 0.0 copy-done
  18.5 0.6 shard_map.149
  19.1 2.2 %collective-permute-start = (f32[16,16,512]{2,1,0:T(8,128)S(1)}, f32[16,16,512]{2,1,0:T(8,128)S(1)}, u32[]{:S(2)}, u32[]{:S(2)}) collective-permute-start(f32[16,16,512]{2,1,0:T(8,128)S(1)} %get-tuple-element.16), channel_id=1, source_target_pairs={{0,1},{1,0},{2,3},{3,2},{4,5},{5,4},{6,7},{7,6},{8,9},{9,8},{10,11... | collective-permute-start | bytes 1572872 | tf_op jit(solution)/shard_map/ppermute | solution.py:28
  21.3 0.4 shard_map.150.a
  21.6 1.2 %collective-permute-done.b = f32[16,16,512]{2,1,0:T(8,128)S(1)} collective-permute-done((f32[16,16,512]{2,1,0:T(8,128)S(1)}, f32[16,16,512]{2,1,0:T(8,128)S(1)}, u32[]{:S(2)}, u32[]{:S(2)}) %collective-permute-start) | collective-permute-done | bytes 524320 | tf_op jit(solution)/shard_map/ppermute | solution.py:28
  22.8 0.1 shard_map.151
  22.9 13.4 %all_to_all.21.parts = f32[16,16,512]{2,1,0:T(8,128)S(1)} all-to-all(f32[16,16,512]{2,1,0:T(8,128)S(1)} %shard_map.151), channel_id=1, replica_groups=mesh['kvp'=16,'tp'=8] {'kvp'}, dimensions={0} | all-to-all | bytes 1048576 | tf_op jit(solution)/shard_map/all_to_all | solution.py:24
  36.3 0.0 slice-start.1
  36.3 0.0 slice-start.3
  36.3 0.0 copy-start.1
  36.4 0.0 copy-start.2
  36.4 4.5 %collective-permute-start.3 = (f32[16,512]{1,0:T(8,128)S(1)}, f32[16,512]{1,0:T(8,128)S(1)}, u32[]{:S(2)}, u32[]{:S(2)}) collective-permute-start(f32[16,512]{1,0:T(8,128)S(1)} %shard_map.152.own), channel_id=1, source_target_pairs={{0,7},{1,6},{2,5},{3,4},{4,3},{5,2},{6,1},{7,0},{8,15},{9,14},{10,... | collective-permute-start | bytes 98312 | tf_op jit(solution)/shard_map/ppermute | solution.py:28
  40.8 0.3 collective-permute-start.2
  41.2 0.6 collective-permute-start.1
  41.8 0.6 collective-permute-done.3.three
  42.4 2.7 %collective-permute-done.2.two = f32[16,512]{1,0:T(8,128)S(1)} collective-permute-done((f32[16,512]{1,0:T(8,128)S(1)}, f32[16,512]{1,0:T(8,128)S(1)}, u32[]{:S(2)}, u32[]{:S(2)}) %collective-permute-start.2) | collective-permute-done | bytes 32800 | tf_op jit(solution)/shard_map/ppermute | solution.py:28
  45.1 0.0 collective-permute-done.1.one
  45.1 0.1 collective-permute-start.4
  45.2 0.0 slice-done
  45.2 0.0 slice-done.2
  45.2 0.0 slice-done.1
  45.2 0.0 slice-done.3
  45.3 0.0 copy-done.1
  45.3 0.0 copy-done.2
  45.3 1.0 %shard_map.154 = (f32[16,512]{1,0:T(8,128)S(1)}, f32[16,3328]{1,0:T(8,128)S(1)}, f32[16,3328]{1,0:T(8,128)S(1)}) custom-call(f32[16,512]{1,0:T(8,128)S(1)} %shard_map.153.own, bf16[4,4,1024]{2,1,0:T(4,128)(2,1)S(1)} %copy-done.1, f32[1,1024]{1,0:T(1,128)S(1)} %bitcast.18, bf16[1024,3328]{1,0:T(8,128)(2,1)S(1)} %bitcast.11, bf16[1024,3328]{1,0:T(8,128)(2,1)S(1)} %bitcast.13), custom_call_target="tpu_custom_call" | custom-call | flops 10000000000 | bytes 14159872 | tf_op jit(solution)/shard_map/pallas_call | solution.py:46
  46.3 0.1 collective-permute-done.4.got
  46.4 1.1 %shard_map.155 = (f32[16,1024]{1,0:T(8,128)S(1)}, f32[16,8,896]{2,1,0:T(8,128)S(1)}) custom-call(f32[16,512]{1,0:T(8,128)S(1)} %collective-permute-done.4.got, f32[16,512]{1,0:T(8,128)S(1)} %get-tuple-element.17.mine_ref, bf16[4,4,1024]{2,1,0:T(4,128)(2,1)S(1)} %copy-done.1, f32[1,1024]{1,0:T(1,128)S(1)} %bitcast.19, bf16[1024,3328]{1,0:T(8,128)(2,1)S(1)} %bitcast.11, ...), custom_call_target="tpu_custom_call" | custom-call | flops 10000000000 | bytes 14684160 | tf_op jit(solution)/shard_map/pallas_call | solution.py:46
  47.5 0.0 slice-start.5
  47.5 13.6 %all_to_all.22.parts = f32[16,8,896]{2,1,0:T(8,128)S(1)} all-to-all(f32[16,8,896]{2,1,0:T(8,128)S(1)} %get-tuple-element.20), channel_id=1, replica_groups=mesh['kvp'=16,'tp'=8] {'kvp'}, dimensions={0} | all-to-all | bytes 917504 | tf_op jit(solution)/shard_map/all_to_all | solution.py:24
  61.2 0.2 shard_map.156
  61.3 10.7 %all_to_all.23.parts = f32[16,8,512]{2,1,0:T(8,128)S(1)} all-to-all(f32[16,8,512]{2,1,0:T(8,128)S(1)} %shard_map.156), channel_id=1, replica_groups=mesh['kvp'=16,'tp'=8] {'kvp'}, dimensions={0} | all-to-all | bytes 524288 | tf_op jit(solution)/shard_map/all_to_all | solution.py:24
  72.1 0.0 slice-done.4
  72.1 0.6 shard_map.157
  72.7 2.4 %collective-permute-start.5 = (f32[16,512]{1,0:T(8,128)S(1)}, f32[16,512]{1,0:T(8,128)S(1)}, u32[]{:S(2)}, u32[]{:S(2)}) collective-permute-start(f32[16,512]{1,0:T(8,128)S(1)} %get-tuple-element.22), channel_id=1, source_target_pairs={{0,1},{1,0},{2,3},{3,2},{4,5},{5,4},{6,7},{7,6},{8,9},{9,8},{10,11... | collective-permute-start | bytes 98312 | tf_op jit(solution)/shard_map/ppermute | solution.py:28
  75.1 0.6 shard_map.158.a
  75.6 0.3 collective-permute-done.5.b
  75.9 1.1 %collective-permute-start.8 = (f32[16,512]{1,0:T(8,128)S(1)}, f32[16,512]{1,0:T(8,128)S(1)}, u32[]{:S(2)}, u32[]{:S(2)}) collective-permute-start(f32[16,512]{1,0:T(8,128)S(1)} %shard_map.159.own), channel_id=1, source_target_pairs={{0,7},{1,6},{2,5},{3,4},{4,3},{5,2},{6,1},{7,0},{8,15},{9,14},{10,... | collective-permute-start | bytes 98312 | tf_op jit(solution)/shard_map/ppermute | solution.py:28
  77.0 0.8 collective-permute-start.7
  77.8 1.9 %collective-permute-start.6 = (f32[16,512]{1,0:T(8,128)S(1)}, f32[16,512]{1,0:T(8,128)S(1)}, u32[]{:S(2)}, u32[]{:S(2)}) collective-permute-start(f32[16,512]{1,0:T(8,128)S(1)} %shard_map.159.own), channel_id=1, source_target_pairs={{0,3},{1,2},{2,1},{3,0},{4,7},{5,6},{6,5},{7,4},{8,11},{9,10},{10,... | collective-permute-start | bytes 98312 | tf_op jit(solution)/shard_map/ppermute | solution.py:28
  79.7 0.7 collective-permute-done.8.three
  80.5 0.8 collective-permute-done.7.two
  81.3 0.8 collective-permute-done.6.one
  82.1 0.6 collective-permute-start.9
  82.7 0.9 %collective-permute-done.9.got = f32[16,512]{1,0:T(8,128)S(1)} collective-permute-done((f32[16,512]{1,0:T(8,128)S(1)}, f32[16,512]{1,0:T(8,128)S(1)}, u32[]{:S(2)}, u32[]{:S(2)}) %collective-permute-start.9) | collective-permute-done | bytes 32800 | tf_op jit(solution)/shard_map/ppermute | solution.py:28
  83.6 0.6 shard_map.161
  (11 shorter events, 0.1 us)
Async XLA Ops:
  0.6 17.9 %copy-start = (bf16[1,1,128,16384]{3,2,1,0:T(8,128)(2,1)S(1)}, bf16[1,1,128,16384]{3,2,1,0:T(8,128)(2,1)}, u32[]{:S(2)}) copy-start(bf16[1,1,128,16384]{3,2,1,0:T(8,128)(2,1)} %param.22) | copy-start | bytes 12582916
  19.1 3.7 %collective-permute-start = (f32[16,16,512]{2,1,0:T(8,128)S(1)}, f32[16,16,512]{2,1,0:T(8,128)S(1)}, u32[]{:S(2)}, u32[]{:S(2)}) collective-permute-start(f32[16,16,512]{2,1,0:T(8,128)S(1)} %get-tuple-element.16), channel_id=1, source_target_pairs={{0,1},{1,0},{2,3},{3,2},{4,5},{5,4},{6,7},{7,6},{8,9},{9,8},{10,11... | collective-permute-start | bytes 1572872 | tf_op jit(solution)/shard_map/ppermute | solution.py:28
  36.3 8.9 %slice-start = ((s8[6815744]{0:T(1024)(128)(4,1)}), s8[4194304]{0:T(1024)(128)(4,1)S(1)}, s32[]{:S(2)}) async-start(s8[6815744]{0:T(1024)(128)(4,1)} %bitcast.10), calls=%async_computation.4 | async-start | bytes 8388608
  36.3 9.0 %slice-start.2 = ((s8[6815744]{0:T(1024)(128)(4,1)}), s8[4194304]{0:T(1024)(128)(4,1)S(1)}, s32[]{:S(2)}) async-start(s8[6815744]{0:T(1024)(128)(4,1)} %bitcast.12), calls=%async_computation.6 | async-start | bytes 8388608
  36.3 8.9 %slice-start.1 = ((s8[6815744]{0:T(1024)(128)(4,1)}), s8[2621440]{0:T(1024)(128)(4,1)S(1)}, s32[]{:S(2)}) async-start(s8[6815744]{0:T(1024)(128)(4,1)} %bitcast.10), calls=%async_computation.5 | async-start | bytes 5242880
  36.3 8.9 %slice-start.3 = ((s8[6815744]{0:T(1024)(128)(4,1)}), s8[2621440]{0:T(1024)(128)(4,1)S(1)}, s32[]{:S(2)}) async-start(s8[6815744]{0:T(1024)(128)(4,1)} %bitcast.12), calls=%async_computation.7 | async-start | bytes 5242880
  36.3 8.9 %copy-start.1 = (bf16[4,4,1024]{2,1,0:T(4,128)(2,1)S(1)}, bf16[4,4,1024]{2,1,0:T(4,128)(2,1)}, u32[]{:S(2)}) copy-start(bf16[4,4,1024]{2,1,0:T(4,128)(2,1)} %res_ref.3) | copy-start | bytes 98308
  36.4 8.9 %copy-start.2 = (f32[1024]{0:T(1024)S(1)}, f32[1024]{0:T(1024)}, u32[]{:S(2)}) copy-start(f32[1024]{0:T(1024)} %param.21) | copy-start | bytes 12292
  36.4 6.1 %collective-permute-start.3 = (f32[16,512]{1,0:T(8,128)S(1)}, f32[16,512]{1,0:T(8,128)S(1)}, u32[]{:S(2)}, u32[]{:S(2)}) collective-permute-start(f32[16,512]{1,0:T(8,128)S(1)} %shard_map.152.own), channel_id=1, source_target_pairs={{0,7},{1,6},{2,5},{3,4},{4,3},{5,2},{6,1},{7,0},{8,15},{9,14},{10,... | collective-permute-start | bytes 98312 | tf_op jit(solution)/shard_map/ppermute | solution.py:28
  40.8 4.3 %collective-permute-start.2 = (f32[16,512]{1,0:T(8,128)S(1)}, f32[16,512]{1,0:T(8,128)S(1)}, u32[]{:S(2)}, u32[]{:S(2)}) collective-permute-start(f32[16,512]{1,0:T(8,128)S(1)} %shard_map.152.own), channel_id=1, source_target_pairs={{0,4},{1,5},{2,6},{3,7},{4,0},{5,1},{6,2},{7,3},{8,12},{9,13},{10,... | collective-permute-start | bytes 98312 | tf_op jit(solution)/shard_map/ppermute | solution.py:28
  41.2 3.9 %collective-permute-start.1 = (f32[16,512]{1,0:T(8,128)S(1)}, f32[16,512]{1,0:T(8,128)S(1)}, u32[]{:S(2)}, u32[]{:S(2)}) collective-permute-start(f32[16,512]{1,0:T(8,128)S(1)} %shard_map.152.own), channel_id=1, source_target_pairs={{0,3},{1,2},{2,1},{3,0},{4,7},{5,6},{6,5},{7,4},{8,11},{9,10},{10,... | collective-permute-start | bytes 98312 | tf_op jit(solution)/shard_map/ppermute | solution.py:28
  45.1 1.3 %collective-permute-start.4 = (f32[16,512]{1,0:T(8,128)S(1)}, f32[16,512]{1,0:T(8,128)S(1)}, u32[]{:S(2)}, u32[]{:S(2)}) collective-permute-start(f32[16,512]{1,0:T(8,128)S(1)} %shard_map.153.own), channel_id=1, source_target_pairs={{0,1},{1,0},{2,3},{3,2},{4,5},{5,4},{6,7},{7,6},{8,9},{9,8},{10,11... | collective-permute-start | bytes 98312 | tf_op jit(solution)/shard_map/ppermute | solution.py:28
  46.4 25.7 %slice-start.4 = ((s8[6815744]{0:T(1024)(128)(4,1)}), s8[4194304]{0:T(1024)(128)(4,1)S(1)}, s32[]{:S(2)}) async-start(s8[6815744]{0:T(1024)(128)(4,1)} %bitcast.14), calls=%async_computation.8 | async-start | bytes 8388608
  47.5 24.6 %slice-start.5 = ((s8[6815744]{0:T(1024)(128)(4,1)}), s8[2621440]{0:T(1024)(128)(4,1)S(1)}, s32[]{:S(2)}) async-start(s8[6815744]{0:T(1024)(128)(4,1)} %bitcast.14), calls=%async_computation.9 | async-start | bytes 5242880
  72.7 3.3 %collective-permute-start.5 = (f32[16,512]{1,0:T(8,128)S(1)}, f32[16,512]{1,0:T(8,128)S(1)}, u32[]{:S(2)}, u32[]{:S(2)}) collective-permute-start(f32[16,512]{1,0:T(8,128)S(1)} %get-tuple-element.22), channel_id=1, source_target_pairs={{0,1},{1,0},{2,3},{3,2},{4,5},{5,4},{6,7},{7,6},{8,9},{9,8},{10,11... | collective-permute-start | bytes 98312 | tf_op jit(solution)/shard_map/ppermute | solution.py:28
  75.9 4.6 %collective-permute-start.8 = (f32[16,512]{1,0:T(8,128)S(1)}, f32[16,512]{1,0:T(8,128)S(1)}, u32[]{:S(2)}, u32[]{:S(2)}) collective-permute-start(f32[16,512]{1,0:T(8,128)S(1)} %shard_map.159.own), channel_id=1, source_target_pairs={{0,7},{1,6},{2,5},{3,4},{4,3},{5,2},{6,1},{7,0},{8,15},{9,14},{10,... | collective-permute-start | bytes 98312 | tf_op jit(solution)/shard_map/ppermute | solution.py:28
  77.0 4.3 %collective-permute-start.7 = (f32[16,512]{1,0:T(8,128)S(1)}, f32[16,512]{1,0:T(8,128)S(1)}, u32[]{:S(2)}, u32[]{:S(2)}) collective-permute-start(f32[16,512]{1,0:T(8,128)S(1)} %shard_map.159.own), channel_id=1, source_target_pairs={{0,4},{1,5},{2,6},{3,7},{4,0},{5,1},{6,2},{7,3},{8,12},{9,13},{10,... | collective-permute-start | bytes 98312 | tf_op jit(solution)/shard_map/ppermute | solution.py:28
  77.8 4.3 %collective-permute-start.6 = (f32[16,512]{1,0:T(8,128)S(1)}, f32[16,512]{1,0:T(8,128)S(1)}, u32[]{:S(2)}, u32[]{:S(2)}) collective-permute-start(f32[16,512]{1,0:T(8,128)S(1)} %shard_map.159.own), channel_id=1, source_target_pairs={{0,3},{1,2},{2,1},{3,0},{4,7},{5,6},{6,5},{7,4},{8,11},{9,10},{10,... | collective-permute-start | bytes 98312 | tf_op jit(solution)/shard_map/ppermute | solution.py:28
  82.1 1.5 %collective-permute-start.9 = (f32[16,512]{1,0:T(8,128)S(1)}, f32[16,512]{1,0:T(8,128)S(1)}, u32[]{:S(2)}, u32[]{:S(2)}) collective-permute-start(f32[16,512]{1,0:T(8,128)S(1)} %shard_map.160.own), channel_id=1, source_target_pairs={{0,1},{1,0},{2,3},{3,2},{4,5},{5,4},{6,7},{7,6},{8,9},{9,8},{10,11... | collective-permute-start | bytes 98312 | tf_op jit(solution)/shard_map/ppermute | solution.py:28

commit v2 on v1

--- a/solution.py
+++ b/solution.py
@@ -84,7 +84,7 @@
     contract = (((1,), (1,)), ((), ()))
     for copy in small + keys:
         copy.wait()
-    stats, weights, fresh_weights = [], [], []
+    stats, weights, fresh_weights = jnp.zeros((rows, dim), F32), [], []
     for s in range(seqs):
         length, owner = len_ref[s], own_ref[s]
         offset = (owner - length) & (KVP - 1)
@@ -107,21 +107,17 @@
         total = total + jnp.sum(fresh_weight, axis=1, keepdims=True)
         weights.append(weight.astype(BF16))
         fresh_weights.append(fresh_weight.astype(BF16))
-        at = 2 * (s // 2)
-        top = top * exponent
-        stats.append(jnp.where(lane == at, top, jnp.where(lane == at + 1, total, 0.0)))
+        stats = jnp.where(lane == 2 * s, top * exponent, stats)
+        stats = jnp.where(lane == 2 * s + 1, total, stats)
     for copy in values:
         copy.wait()
     for s in range(seqs):
         sums = jnp.dot(weights[s], v_ref[s], preferred_element_type=F32)
         sums = sums + jnp.dot(fresh_weights[s], vn_ref[...], preferred_element_type=F32)
         for h in range(rows // drafts):
-            packed[h, drafts * s : drafts * (s + 1), :] = sums[drafts * h : drafts * (h + 1), :]
-    for part in range(2):
-        both = stats[part] + stats[part + 2]
-        base = 16 + drafts * part
-        for h in range(rows // drafts):
-            packed[h, base : base + drafts, :] = both[drafts * h : drafts * (h + 1), :]
+            packed[h, s] = sums[drafts * h : drafts * (h + 1), :]
+    for h in range(rows // drafts):
+        packed[h, seqs] = stats[drafts * h : drafts * (h + 1), :]
 
 
 def project(att, w_ref, out_ref, half):
@@ -132,15 +128,15 @@
 
 
 def project_other_kernel(parts, w_ref, att_ref, out_ref):
-    halves = []
-    for half in range(2):
-        tops = parts[:, 16:24, 2 * half : 2 * half + 1]
-        totals = parts[:, 16:24, 2 * half + 1 : 2 * half + 2]
+    pieces = []
+    seqs = parts.shape[1] - 1
+    for s in range(seqs):
+        tops = parts[:, seqs, :, 2 * s : 2 * s + 1]
+        totals = parts[:, seqs, :, 2 * s + 1 : 2 * s + 2]
         scales = jnp.exp2(tops - jnp.max(tops, axis=0, keepdims=True))
         total = jnp.sum(totals * scales, axis=0)
-        sums = jnp.sum(parts[:, 8 * half : 8 * half + 8, :] * scales, axis=0)
-        halves.append(sums / total)
-    att = jnp.concatenate(halves, axis=0).astype(BF16)
+        pieces.append(jnp.sum(parts[:, s] * scales, axis=0) / total)
+    att = jnp.concatenate(pieces, axis=0).astype(BF16)
     att_ref[...] = att
     project(att, w_ref, out_ref, 1 - half_here())
 
@@ -251,10 +247,13 @@
     factor = lax.rsqrt(mixed[:, 64:65] / D + EPSILON)
     active = gated(total[:, :384] * factor, total[:, 384:768] * factor)
     extra = gated(mixed[:, :32] * factor, mixed[:, 32:64] * factor)
-    extra = jnp.concatenate([extra, jnp.zeros((8, 96), F32)], axis=1)
+    extra = jnp.concatenate([extra[:4], extra[4:], jnp.zeros((4, 64), F32)], axis=1)
     for i in range(out.shape[0]):
-        out[i, :, :384] = active
-        out[i, :, 384:] = extra
+        for block in range(3):
+            columns = slice(128 * block, 128 * (block + 1))
+            out[i, 2 * block] = active[:4, columns]
+            out[i, 2 * block + 1] = active[4:, columns]
+        out[i, 6] = extra
 
 
 def down(active, w_ref, out, half):
@@ -269,9 +268,14 @@
 def down_other_kernel(parts, w_ref, active_ref, out):
     halves = []
     for r in range(2):
-        pairs = [parts[2 * p + r] for p in range(KVP // 2)]
-        columns = [p[:, :384] for p in pairs] + [p[:, 384:416] for p in pairs]
-        halves.append(jnp.concatenate(columns, axis=1))
+        columns, extras = [], []
+        for member in range(r, KVP, 2):
+            for block in range(3):
+                rows = [parts[member, 2 * block], parts[member, 2 * block + 1]]
+                columns.append(jnp.concatenate(rows, axis=0))
+            last = parts[member, 6]
+            extras.append(jnp.concatenate([last[:, :32], last[:, 32:64]], axis=0))
+        halves.append(jnp.concatenate(columns + extras, axis=1))
     active = jnp.concatenate(halves, axis=0).astype(BF16)
     active_ref[...] = active
     down(active, w_ref, out, 1 - half_here())
@@ -326,7 +330,7 @@
     ]
     (parts,) = call(
         attention_kernel,
-        [shaped((KVP, 24, dim))],
+        [shaped((KVP, seqs + 1, drafts, dim))],
         in_hbm,
         scratch=[
             pltpu.SMEM((seqs,), jnp.int32),
@@ -368,7 +372,7 @@
         flops=FLOPS,
     )
     (parts,) = call(
-        active_kernel, [shaped((KVP, 8, 512))], [exchange(parts, "kvp")], flops=FLOPS
+        active_kernel, [shaped((KVP, 7, 4, 128))], [exchange(parts, "kvp")], flops=FLOPS
     )
     active, theirs = call(
         down_other_kernel,

time: 84.4 us -> 84.3 us (level)
  no operation moved by 1% of the time
where the time goes in v2:
time: 84.3 us; the launch traced here: 84.1 us
  blocking collectives  52.8 us (63%)
  starting transfers between devices  14.6 us (17%)
  waiting for transfers between devices  8.06 us (10%)
  Pallas kernels  7.73 us (9%)
    all_to_all x4, blocking collectives, exchange(): return lax.all_to_all(blocks, axis, split_axis=0, concat_axis=0, tiled=True)  52.8 us
    ppermute x10, starting transfers between devices, permute(): return lax.ppermute(value, 'tp', pairs)  14.6 us
    ppermute x10, waiting for transfers between devices, permute(): return lax.ppermute(value, 'tp', pairs)  8.06 us
    pallas_call x14, Pallas kernels, call(): pl.pallas_call(kernel, out_shape=tuple(outs), in_specs=[pl.BlockSpec(memo...  7.73 us
  transfers between devices with their start and end apart: 10, of which 9 were waited for; matrix products, arithmetic and copies ran while one was open for 0% of the time, Pallas kernels for 2%

profile of v2, /device:TPU:1, one launch (start us, length us, event | category | flops | bytes accessed | tf_op | source)
XLA Modules:
  0.0 84.1 jit_solution(8492460587885657574)
XLA Ops:
  0.6 0.0 copy-start
  0.6 2.5 %shard_map.148 = f32[16,5,4,128]{3,2,1,0:T(4,128)S(1)} custom-call(s32[4]{0:T(128)} %refs_0_.1, s32[4]{0:T(128)} %refs_1_.1, bf16[256,128]{1,0:T(8,128)(2,1)} %bitcast.22, bf16[16,128]{1,0:T(8,128)(2,1)} %bitcast.23, bf16[16,128]{1,0:T(8,128)(2,1)} %bitcast.24, bf16[4,1024,128]{2,1,0:T(8,128)(2,1)} %bitcast.20, bf16[4,1024,128]{2,1,0:T(8,128)(2,1)} %bitcast.21), custom_call_target="tpu_custom_call" | custom-call | flops 10000000000 | bytes 2334752 | tf_op jit(solution)/shard_map/pallas_call | solution.py:46
  3.1 15.2 %all_to_all.20.parts = f32[16,5,4,128]{3,2,1,0:T(4,128)S(1)} all-to-all(f32[16,5,4,128]{3,2,1,0:T(4,128)S(1)} %shard_map.148), channel_id=1, replica_groups=mesh['kvp'=16,'tp'=8] {'kvp'}, dimensions={0} | all-to-all | bytes 327680 | tf_op jit(solution)/shard_map/all_to_all | solution.py:24
  18.4 0.0 copy-done
  18.4 0.6 shard_map.149
  19.0 2.2 %collective-permute-start = (f32[16,16,512]{2,1,0:T(8,128)S(1)}, f32[16,16,512]{2,1,0:T(8,128)S(1)}, u32[]{:S(2)}, u32[]{:S(2)}) collective-permute-start(f32[16,16,512]{2,1,0:T(8,128)S(1)} %get-tuple-element.16), channel_id=1, source_target_pairs={{0,1},{1,0},{2,3},{3,2},{4,5},{5,4},{6,7},{7,6},{8,9},{9,8},{10,11... | collective-permute-start | bytes 1572872 | tf_op jit(solution)/shard_map/ppermute | solution.py:28
  21.2 0.4 shard_map.150.a
  21.5 1.2 %collective-permute-done.b = f32[16,16,512]{2,1,0:T(8,128)S(1)} collective-permute-done((f32[16,16,512]{2,1,0:T(8,128)S(1)}, f32[16,16,512]{2,1,0:T(8,128)S(1)}, u32[]{:S(2)}, u32[]{:S(2)}) %collective-permute-start) | collective-permute-done | bytes 524320 | tf_op jit(solution)/shard_map/ppermute | solution.py:28
  22.7 0.1 shard_map.151
  22.8 13.5 %all_to_all.21.parts = f32[16,16,512]{2,1,0:T(8,128)S(1)} all-to-all(f32[16,16,512]{2,1,0:T(8,128)S(1)} %shard_map.151), channel_id=1, replica_groups=mesh['kvp'=16,'tp'=8] {'kvp'}, dimensions={0} | all-to-all | bytes 1048576 | tf_op jit(solution)/shard_map/all_to_all | solution.py:24
  36.3 0.0 slice-start.1
  36.3 0.0 slice-start.3
  36.3 0.0 copy-start.1
  36.3 0.0 copy-start.2
  36.3 4.5 %collective-permute-start.3 = (f32[16,512]{1,0:T(8,128)S(1)}, f32[16,512]{1,0:T(8,128)S(1)}, u32[]{:S(2)}, u32[]{:S(2)}) collective-permute-start(f32[16,512]{1,0:T(8,128)S(1)} %shard_map.152.own), channel_id=1, source_target_pairs={{0,7},{1,6},{2,5},{3,4},{4,3},{5,2},{6,1},{7,0},{8,15},{9,14},{10,... | collective-permute-start | bytes 98312 | tf_op jit(solution)/shard_map/ppermute | solution.py:28
  40.8 0.3 collective-permute-start.2
  41.1 0.6 collective-permute-start.1
  41.7 0.6 collective-permute-done.3.three
  42.4 2.7 %collective-permute-done.2.two = f32[16,512]{1,0:T(8,128)S(1)} collective-permute-done((f32[16,512]{1,0:T(8,128)S(1)}, f32[16,512]{1,0:T(8,128)S(1)}, u32[]{:S(2)}, u32[]{:S(2)}) %collective-permute-start.2) | collective-permute-done | bytes 32800 | tf_op jit(solution)/shard_map/ppermute | solution.py:28
  45.1 0.0 collective-permute-done.1.one
  45.1 0.1 collective-permute-start.4
  45.2 0.0 slice-done
  45.2 0.0 slice-done.2
  45.2 0.0 slice-done.1
  45.2 0.0 slice-done.3
  45.2 0.0 copy-done.1
  45.2 0.0 copy-done.2
  45.2 1.0 %shard_map.154 = (f32[16,512]{1,0:T(8,128)S(1)}, f32[16,3328]{1,0:T(8,128)S(1)}, f32[16,3328]{1,0:T(8,128)S(1)}) custom-call(f32[16,512]{1,0:T(8,128)S(1)} %shard_map.153.own, bf16[4,4,1024]{2,1,0:T(4,128)(2,1)S(1)} %copy-done.1, f32[1,1024]{1,0:T(1,128)S(1)} %bitcast.18, bf16[1024,3328]{1,0:T(8,128)(2,1)S(1)} %bitcast.11, bf16[1024,3328]{1,0:T(8,128)(2,1)S(1)} %bitcast.13), custom_call_target="tpu_custom_call" | custom-call | flops 10000000000 | bytes 14159872 | tf_op jit(solution)/shard_map/pallas_call | solution.py:46
  46.2 0.1 collective-permute-done.4.got
  46.4 1.1 %shard_map.155 = (f32[16,1024]{1,0:T(8,128)S(1)}, f32[16,8,896]{2,1,0:T(8,128)S(1)}) custom-call(f32[16,512]{1,0:T(8,128)S(1)} %collective-permute-done.4.got, f32[16,512]{1,0:T(8,128)S(1)} %get-tuple-element.17.mine_ref, bf16[4,4,1024]{2,1,0:T(4,128)(2,1)S(1)} %copy-done.1, f32[1,1024]{1,0:T(1,128)S(1)} %bitcast.19, bf16[1024,3328]{1,0:T(8,128)(2,1)S(1)} %bitcast.11, ...), custom_call_target="tpu_custom_call" | custom-call | flops 10000000000 | bytes 14684160 | tf_op jit(solution)/shard_map/pallas_call | solution.py:46
  47.5 0.0 slice-start.5
  47.5 13.6 %all_to_all.22.parts = f32[16,8,896]{2,1,0:T(8,128)S(1)} all-to-all(f32[16,8,896]{2,1,0:T(8,128)S(1)} %get-tuple-element.20), channel_id=1, replica_groups=mesh['kvp'=16,'tp'=8] {'kvp'}, dimensions={0} | all-to-all | bytes 917504 | tf_op jit(solution)/shard_map/all_to_all | solution.py:24
  61.1 0.2 shard_map.156
  61.4 10.5 %all_to_all.23.parts = f32[16,7,4,128]{3,2,1,0:T(4,128)S(1)} all-to-all(f32[16,7,4,128]{3,2,1,0:T(4,128)S(1)} %shard_map.156), channel_id=1, replica_groups=mesh['kvp'=16,'tp'=8] {'kvp'}, dimensions={0} | all-to-all | bytes 458752 | tf_op jit(solution)/shard_map/all_to_all | solution.py:24
  71.8 0.0 slice-done.4
  71.8 0.6 shard_map.157
  72.4 2.5 %collective-permute-start.5 = (f32[16,512]{1,0:T(8,128)S(1)}, f32[16,512]{1,0:T(8,128)S(1)}, u32[]{:S(2)}, u32[]{:S(2)}) collective-permute-start(f32[16,512]{1,0:T(8,128)S(1)} %get-tuple-element.22), channel_id=1, source_target_pairs={{0,1},{1,0},{2,3},{3,2},{4,5},{5,4},{6,7},{7,6},{8,9},{9,8},{10,11... | collective-permute-start | bytes 98312 | tf_op jit(solution)/shard_map/ppermute | solution.py:28
  74.9 0.6 shard_map.158.a
  75.5 0.3 collective-permute-done.5.b
  75.8 1.1 %collective-permute-start.8 = (f32[16,512]{1,0:T(8,128)S(1)}, f32[16,512]{1,0:T(8,128)S(1)}, u32[]{:S(2)}, u32[]{:S(2)}) collective-permute-start(f32[16,512]{1,0:T(8,128)S(1)} %shard_map.159.own), channel_id=1, source_target_pairs={{0,7},{1,6},{2,5},{3,4},{4,3},{5,2},{6,1},{7,0},{8,15},{9,14},{10,... | collective-permute-start | bytes 98312 | tf_op jit(solution)/shard_map/ppermute | solution.py:28
  76.9 0.8 collective-permute-start.7
  77.7 1.9 %collective-permute-start.6 = (f32[16,512]{1,0:T(8,128)S(1)}, f32[16,512]{1,0:T(8,128)S(1)}, u32[]{:S(2)}, u32[]{:S(2)}) collective-permute-start(f32[16,512]{1,0:T(8,128)S(1)} %shard_map.159.own), channel_id=1, source_target_pairs={{0,3},{1,2},{2,1},{3,0},{4,7},{5,6},{6,5},{7,4},{8,11},{9,10},{10,... | collective-permute-start | bytes 98312 | tf_op jit(solution)/shard_map/ppermute | solution.py:28
  79.6 0.7 collective-permute-done.8.three
  80.3 0.8 collective-permute-done.7.two
  81.1 0.8 collective-permute-done.6.one
  81.9 0.6 collective-permute-start.9
  82.6 0.9 %collective-permute-done.9.got = f32[16,512]{1,0:T(8,128)S(1)} collective-permute-done((f32[16,512]{1,0:T(8,128)S(1)}, f32[16,512]{1,0:T(8,128)S(1)}, u32[]{:S(2)}, u32[]{:S(2)}) %collective-permute-start.9) | collective-permute-done | bytes 32800 | tf_op jit(solution)/shard_map/ppermute | solution.py:28
  83.4 0.6 shard_map.161
  (11 shorter events, 0.1 us)
Async XLA Ops:
  0.6 17.7 %copy-start = (bf16[1,1,128,16384]{3,2,1,0:T(8,128)(2,1)S(1)}, bf16[1,1,128,16384]{3,2,1,0:T(8,128)(2,1)}, u32[]{:S(2)}) copy-start(bf16[1,1,128,16384]{3,2,1,0:T(8,128)(2,1)} %param.22) | copy-start | bytes 12582916
  19.0 3.7 %collective-permute-start = (f32[16,16,512]{2,1,0:T(8,128)S(1)}, f32[16,16,512]{2,1,0:T(8,128)S(1)}, u32[]{:S(2)}, u32[]{:S(2)}) collective-permute-start(f32[16,16,512]{2,1,0:T(8,128)S(1)} %get-tuple-element.16), channel_id=1, source_target_pairs={{0,1},{1,0},{2,3},{3,2},{4,5},{5,4},{6,7},{7,6},{8,9},{9,8},{10,11... | collective-permute-start | bytes 1572872 | tf_op jit(solution)/shard_map/ppermute | solution.py:28
  36.2 8.9 %slice-start = ((s8[6815744]{0:T(1024)(128)(4,1)}), s8[4194304]{0:T(1024)(128)(4,1)S(1)}, s32[]{:S(2)}) async-start(s8[6815744]{0:T(1024)(128)(4,1)} %bitcast.10), calls=%async_computation.4 | async-start | bytes 8388608
  36.2 8.9 %slice-start.2 = ((s8[6815744]{0:T(1024)(128)(4,1)}), s8[4194304]{0:T(1024)(128)(4,1)S(1)}, s32[]{:S(2)}) async-start(s8[6815744]{0:T(1024)(128)(4,1)} %bitcast.12), calls=%async_computation.6 | async-start | bytes 8388608
  36.3 8.9 %slice-start.1 = ((s8[6815744]{0:T(1024)(128)(4,1)}), s8[2621440]{0:T(1024)(128)(4,1)S(1)}, s32[]{:S(2)}) async-start(s8[6815744]{0:T(1024)(128)(4,1)} %bitcast.10), calls=%async_computation.5 | async-start | bytes 5242880
  36.3 8.9 %slice-start.3 = ((s8[6815744]{0:T(1024)(128)(4,1)}), s8[2621440]{0:T(1024)(128)(4,1)S(1)}, s32[]{:S(2)}) async-start(s8[6815744]{0:T(1024)(128)(4,1)} %bitcast.12), calls=%async_computation.7 | async-start | bytes 5242880
  36.3 8.9 %copy-start.1 = (bf16[4,4,1024]{2,1,0:T(4,128)(2,1)S(1)}, bf16[4,4,1024]{2,1,0:T(4,128)(2,1)}, u32[]{:S(2)}) copy-start(bf16[4,4,1024]{2,1,0:T(4,128)(2,1)} %res_ref.3) | copy-start | bytes 98308
  36.3 8.9 %copy-start.2 = (f32[1024]{0:T(1024)S(1)}, f32[1024]{0:T(1024)}, u32[]{:S(2)}) copy-start(f32[1024]{0:T(1024)} %param.21) | copy-start | bytes 12292
  36.3 6.1 %collective-permute-start.3 = (f32[16,512]{1,0:T(8,128)S(1)}, f32[16,512]{1,0:T(8,128)S(1)}, u32[]{:S(2)}, u32[]{:S(2)}) collective-permute-start(f32[16,512]{1,0:T(8,128)S(1)} %shard_map.152.own), channel_id=1, source_target_pairs={{0,7},{1,6},{2,5},{3,4},{4,3},{5,2},{6,1},{7,0},{8,15},{9,14},{10,... | collective-permute-start | bytes 98312 | tf_op jit(solution)/shard_map/ppermute | solution.py:28
  40.8 4.3 %collective-permute-start.2 = (f32[16,512]{1,0:T(8,128)S(1)}, f32[16,512]{1,0:T(8,128)S(1)}, u32[]{:S(2)}, u32[]{:S(2)}) collective-permute-start(f32[16,512]{1,0:T(8,128)S(1)} %shard_map.152.own), channel_id=1, source_target_pairs={{0,4},{1,5},{2,6},{3,7},{4,0},{5,1},{6,2},{7,3},{8,12},{9,13},{10,... | collective-permute-start | bytes 98312 | tf_op jit(solution)/shard_map/ppermute | solution.py:28
  41.1 3.9 %collective-permute-start.1 = (f32[16,512]{1,0:T(8,128)S(1)}, f32[16,512]{1,0:T(8,128)S(1)}, u32[]{:S(2)}, u32[]{:S(2)}) collective-permute-start(f32[16,512]{1,0:T(8,128)S(1)} %shard_map.152.own), channel_id=1, source_target_pairs={{0,3},{1,2},{2,1},{3,0},{4,7},{5,6},{6,5},{7,4},{8,11},{9,10},{10,... | collective-permute-start | bytes 98312 | tf_op jit(solution)/shard_map/ppermute | solution.py:28
  45.1 1.3 %collective-permute-start.4 = (f32[16,512]{1,0:T(8,128)S(1)}, f32[16,512]{1,0:T(8,128)S(1)}, u32[]{:S(2)}, u32[]{:S(2)}) collective-permute-start(f32[16,512]{1,0:T(8,128)S(1)} %shard_map.153.own), channel_id=1, source_target_pairs={{0,1},{1,0},{2,3},{3,2},{4,5},{5,4},{6,7},{7,6},{8,9},{9,8},{10,11... | collective-permute-start | bytes 98312 | tf_op jit(solution)/shard_map/ppermute | solution.py:28
  46.4 25.5 %slice-start.4 = ((s8[6815744]{0:T(1024)(128)(4,1)}), s8[4194304]{0:T(1024)(128)(4,1)S(1)}, s32[]{:S(2)}) async-start(s8[6815744]{0:T(1024)(128)(4,1)} %bitcast.14), calls=%async_computation.8 | async-start | bytes 8388608
  47.5 24.4 %slice-start.5 = ((s8[6815744]{0:T(1024)(128)(4,1)}), s8[2621440]{0:T(1024)(128)(4,1)S(1)}, s32[]{:S(2)}) async-start(s8[6815744]{0:T(1024)(128)(4,1)} %bitcast.14), calls=%async_computation.9 | async-start | bytes 5242880
  72.4 3.3 %collective-permute-start.5 = (f32[16,512]{1,0:T(8,128)S(1)}, f32[16,512]{1,0:T(8,128)S(1)}, u32[]{:S(2)}, u32[]{:S(2)}) collective-permute-start(f32[16,512]{1,0:T(8,128)S(1)} %get-tuple-element.22), channel_id=1, source_target_pairs={{0,1},{1,0},{2,3},{3,2},{4,5},{5,4},{6,7},{7,6},{8,9},{9,8},{10,11... | collective-permute-start | bytes 98312 | tf_op jit(solution)/shard_map/ppermute | solution.py:28
  75.8 4.6 %collective-permute-start.8 = (f32[16,512]{1,0:T(8,128)S(1)}, f32[16,512]{1,0:T(8,128)S(1)}, u32[]{:S(2)}, u32[]{:S(2)}) collective-permute-start(f32[16,512]{1,0:T(8,128)S(1)} %shard_map.159.own), channel_id=1, source_target_pairs={{0,7},{1,6},{2,5},{3,4},{4,3},{5,2},{6,1},{7,0},{8,15},{9,14},{10,... | collective-permute-start | bytes 98312 | tf_op jit(solution)/shard_map/ppermute | solution.py:28
  76.9 4.3 %collective-permute-start.7 = (f32[16,512]{1,0:T(8,128)S(1)}, f32[16,512]{1,0:T(8,128)S(1)}, u32[]{:S(2)}, u32[]{:S(2)}) collective-permute-start(f32[16,512]{1,0:T(8,128)S(1)} %shard_map.159.own), channel_id=1, source_target_pairs={{0,4},{1,5},{2,6},{3,7},{4,0},{5,1},{6,2},{7,3},{8,12},{9,13},{10,... | collective-permute-start | bytes 98312 | tf_op jit(solution)/shard_map/ppermute | solution.py:28
  77.7 4.2 %collective-permute-start.6 = (f32[16,512]{1,0:T(8,128)S(1)}, f32[16,512]{1,0:T(8,128)S(1)}, u32[]{:S(2)}, u32[]{:S(2)}) collective-permute-start(f32[16,512]{1,0:T(8,128)S(1)} %shard_map.159.own), channel_id=1, source_target_pairs={{0,3},{1,2},{2,1},{3,0},{4,7},{5,6},{6,5},{7,4},{8,11},{9,10},{10,... | collective-permute-start | bytes 98312 | tf_op jit(solution)/shard_map/ppermute | solution.py:28
  81.9 1.5 %collective-permute-start.9 = (f32[16,512]{1,0:T(8,128)S(1)}, f32[16,512]{1,0:T(8,128)S(1)}, u32[]{:S(2)}, u32[]{:S(2)}) collective-permute-start(f32[16,512]{1,0:T(8,128)S(1)} %shard_map.160.own), channel_id=1, source_target_pairs={{0,1},{1,0},{2,3},{3,2},{4,5},{5,4},{6,7},{7,6},{8,9},{9,8},{10,11... | collective-permute-start | bytes 98312 | tf_op jit(solution)/shard_map/ppermute | solution.py:28
